TPU v7x, 512 devices: a whole 4x4x16 slice. The times are simulated.
512 devices in a mesh: fsdp: 16 (over z_hi, x), ctx: 32 (over z_lo, y, core).
Axes of the slice: x: 4, y: 4, z: 16 (z_hi: 4, z_lo: 4; z = z_hi * 4 + z_lo), core: 2. Of those that a mesh axis runs over, the one named last changes fastest.
Arguments:
- features: bfloat16 [16, 3, 2048, 8192], P('fsdp', None, None, 'ctx'), may hold values from -6 to 6
- short_taps: bfloat16 [7, 3, 2048], replicated, may hold values from -2 to 2
- filters: bfloat16 [128, 128], replicated, may hold values from -0.5 to 0.5
- out_weight: bfloat16 [2048, 2048], P('fsdp'), may hold values from -0.125 to 0.125
Outputs:
- mixed_out: bfloat16 [16, 8192, 2048], P('fsdp', 'ctx')
All inputs are finite; a program needn't handle non-finite values.
Results may differ from a plain program's by a relative error of at most 0.0058.
Values may be sent and summed in bfloat16 or wider, within the bound.
A program may use at most 128 MiB of HBM per device.

v0:
```python
import jax
import jax.numpy as jnp
from jax import lax
from jax.sharding import PartitionSpec as P

GROUP = 16


def toeplitz(filters):
    groups = filters.shape[0]
    length = filters.shape[1]
    reverse = jnp.concatenate([filters[:, :1], filters[:, :0:-1]], axis=1)
    tiled = jnp.tile(reverse, (1, 2 * length - 1)).reshape(groups, length, 2 * length - 1)[
        :, :, :length
    ]
    row_index = lax.broadcasted_iota(jnp.int32, (length, length), 0)
    col_index = lax.broadcasted_iota(jnp.int32, (length, length), 1)
    lower = jnp.where(row_index >= col_index, tiled, jnp.zeros_like(tiled))
    upper = jnp.where(row_index < col_index, tiled, jnp.zeros_like(tiled))
    return (lower, upper)


def short_conv(padded, weights):
    width = weights.shape[0]
    length = padded.shape[2] - width + 1
    result = weights[0][:, :, None] * padded[:, :, width - 1 : width - 1 + length]
    for offset in range(1, width):
        result = (
            result
            + weights[offset][:, :, None]
            * padded[:, :, width - 1 - offset : width - 1 - offset + length]
        )
    return result


def block_filter(extended, lower, upper):
    channels = extended.shape[0]
    length = lower.shape[1]
    groups = lower.shape[0]
    blocks = extended.shape[1] // length
    shaped = extended.reshape(groups, channels // groups, blocks, length)
    result = jnp.einsum(
        "gtu,gcbu->gcbt", lower, shaped[:, :, 1:], preferred_element_type=jnp.float32
    )
    result = result + jnp.einsum(
        "gtu,gcbu->gcbt", upper, shaped[:, :, :-1], preferred_element_type=jnp.float32
    )
    return result.reshape(channels, (blocks - 1) * length)


def on_device(features, short_taps, filters, out_weight):
    sequence = features[0]
    weights = short_taps.astype(jnp.float32)
    width = weights.shape[0]
    length = filters.shape[1]
    spread = lax.all_to_all(sequence, "ctx", split_axis=1, concat_axis=2, tiled=True)
    channels = spread.shape[1]
    offset_c = lax.axis_index("ctx") * channels
    own_weights = lax.dynamic_slice_in_dim(weights, offset_c, channels, 2)
    group_count = channels // GROUP
    own_filters = lax.dynamic_slice_in_dim(
        filters, lax.axis_index("ctx") * group_count, group_count, 0
    )
    lower, upper = toeplitz(own_filters)
    values = spread.astype(jnp.float32)
    convolved = short_conv(jnp.pad(values, ((0, 0), (0, 0), (width - 1, 0))), own_weights)
    product = (convolved[1] * convolved[2]).astype(jnp.bfloat16)
    filtered = block_filter(jnp.pad(product, ((0, 0), (length, 0))), lower, upper)
    gated = (convolved[0] * filtered).astype(jnp.bfloat16)
    mixed = lax.all_to_all(gated, "ctx", split_axis=1, concat_axis=0, tiled=True)
    result = lax.dot_general(
        mixed,
        lax.all_gather(out_weight, "fsdp", axis=0, tiled=True),
        (((0,), (0,)), ((), ())),
        preferred_element_type=jnp.float32,
    )
    return result.astype(jnp.bfloat16)[None]


def solution(mesh):
    in_specs = (P("fsdp", None, None, "ctx"), P(), P(), P("fsdp", None))
    out_specs = P("fsdp", "ctx", None)
    return jax.shard_map(
        on_device, mesh=mesh, in_specs=in_specs, out_specs=out_specs, check_vma=False
    )
```

profile of v0, /device:TPU:1, one launch (start us, length us, event | category | flops | bytes accessed | tf_op | source)
XLA Modules:
  0.0 370.6 jit_solution(6496001617876004528)
XLA Ops:
  6.5 0.0 copy-start
  6.5 6.8 %copy.31 = bf16[1,3,2048,256]{3,1,2,0:T(4,128)(2,1)} copy(bf16[1,3,2048,256]{3,2,1,0:T(8,128)(2,1)} %param.4) | data formatting | bytes 6291456 | tf_op args[0]
  13.3 11.3 %all-to-all-start = ((bf16[3,2048,256]{2,0,1:T(4,128)(2,1)}), bf16[3,2048,256]{2,0,1:T(4,128)(2,1)}, u32[]{:S(2)}, u32[]{:S(2)}) async-start(bf16[3,2048,256]{2,0,1:T(4,128)(2,1)} %bitcast.52), calls=%async_computation | async-start | bytes 8388608 | tf_op jit(solution)/shard_map/all_to_all | solution.py:56
  24.6 0.0 all-gather.2.cloned.1.call-start
  24.7 0.7 all-gather.2.cloned.1.call-update
  25.4 0.8 dynamic-slice_convert_fusion
  26.2 0.0 copy-done
  26.2 0.1 slice.82
  26.3 0.1 rev.3
  26.4 0.1 pad_maximum_fusion
  26.5 0.8 tile.9
  27.4 232.6 %all-to-all-done = bf16[3,2048,256]{2,0,1:T(4,128)(2,1)} async-done(((bf16[3,2048,256]{2,0,1:T(4,128)(2,1)}), bf16[3,2048,256]{2,0,1:T(4,128)(2,1)}, u32[]{:S(2)}, u32[]{:S(2)}) %all-to-all-start) | async-done | bytes 3145760 | tf_op jit(solution)/shard_map/all_to_all | solution.py:56
  260.0 3.4 convert_bitcast_fusion
  263.4 6.3 %copy.11 = f32[3,64,32,256]{3,2,1,0:T(8,128)} copy(f32[3,64,32,256]{3,0,1,2:T(4,128)S(1)} %convert_bitcast_fusion) | data formatting | bytes 12582912 | tf_op jit(solution)/shard_map/convert_element_type | solution.py:65
  269.8 7.2 %reshape.30 = f32[3,64,8192]{2,1,0:T(8,128)} reshape(f32[3,64,32,256]{3,2,1,0:T(8,128)} %copy.11) | data formatting | bytes 12582912 | tf_op jit(solution)/shard_map/convert_element_type | solution.py:65
  276.9 24.1 %multiply_add_fusion = f32[3,64,8192]{2,1,0:T(8,128)S(1)} fusion(f32[3,64,8192]{2,1,0:T(8,128)} %reshape.30, f32[3,64]{1,0:T(4,128)S(1)} %get-tuple-element.14, f32[3,64]{1,0:T(4,128)S(1)} %get-tuple-element.15, f32[3,64]{1,0:T(4,128)S(1)} %get-tuple-element.16, f32[3,64]{1,0:T(4,128)S(1)} %get-tuple-element.17, f32[3,64]{1,0:T(4,128)S(1)} %get-tuple-element.18, ...), kind=kLoop, calls=%fused_computation.1 | loop fusion | flops 20447232 | bytes 12588288 | tf_op jit(solution)/shard_map/add | solution.py:29
  301.0 1.7 fusion.19
  302.7 0.1 pad.9
  302.7 0.6 reshape.28
  303.3 0.5 fusion.5
  303.8 1.8 convolution_add_fusion
  305.5 1.9 reshape.29
  307.4 2.2 copy.22
  309.6 0.5 fusion.1
  310.2 1.6 copy.12
  311.7 18.8 %all-to-all-start.1 = ((bf16[64,32,256]{2,0,1:T(8,128)(2,1)}), bf16[64,32,256]{2,0,1:T(8,128)(2,1)S(1)}, u32[]{:S(2)}, u32[]{:S(2)}) async-start(bf16[64,32,256]{2,0,1:T(8,128)(2,1)} %copy.12), calls=%async_computation.1 | async-start | bytes 2097152 | tf_op jit(solution)/shard_map/all_to_all | solution.py:70
  330.5 0.0 all-gather.2.cloned.1.call-done
  330.5 26.6 %all-to-all-done.1 = bf16[64,32,256]{2,0,1:T(8,128)(2,1)S(1)} async-done(((bf16[64,32,256]{2,0,1:T(8,128)(2,1)}), bf16[64,32,256]{2,0,1:T(8,128)(2,1)S(1)}, u32[]{:S(2)}, u32[]{:S(2)}) %all-to-all-start.1) | async-done | bytes 1048608 | tf_op jit(solution)/shard_map/all_to_all | solution.py:70
  357.1 6.7 %fusion = bf16[1,256,2048]{2,1,0:T(8,128)(2,1)} fusion(bf16[2048,256]{1,0:T(8,128)(2,1)S(1)} %bitcast.54, bf16[2048,2048]{1,0:T(8,128)(2,1)} %all-gather.2.cloned.1.call-done), kind=kOutput, calls=%fused_computation.4 | convolution fusion | flops 2148007936 | bytes 10485760 | tf_op jit(solution)/shard_map/dot_general | solution.py:71
  (9 shorter events, 0.1 us)
Async XLA Ops:
  6.5 19.6 %copy-start = (bf16[128,128]{1,0:T(8,128)(2,1)S(1)}, bf16[128,128]{1,0:T(8,128)(2,1)}, u32[]{:S(2)}) copy-start(bf16[128,128]{1,0:T(8,128)(2,1)} %param.6) | copy-start | bytes 98308
  13.3 246.7 %all-to-all-start = ((bf16[3,2048,256]{2,0,1:T(4,128)(2,1)}), bf16[3,2048,256]{2,0,1:T(4,128)(2,1)}, u32[]{:S(2)}, u32[]{:S(2)}) async-start(bf16[3,2048,256]{2,0,1:T(4,128)(2,1)} %bitcast.52), calls=%async_computation | async-start | bytes 8388608 | tf_op jit(solution)/shard_map/all_to_all | solution.py:56
  24.6 305.9 %all-gather.2.cloned.1.call-start = ((), (), s32[]{:S(2)}) async-start(), calls=%async_computation.2 | async-start | bytes 8912896 | tf_op jit(solution)/shard_map/all_gather | solution.py:73
  311.7 45.3 %all-to-all-start.1 = ((bf16[64,32,256]{2,0,1:T(8,128)(2,1)}), bf16[64,32,256]{2,0,1:T(8,128)(2,1)S(1)}, u32[]{:S(2)}, u32[]{:S(2)}) async-start(bf16[64,32,256]{2,0,1:T(8,128)(2,1)} %copy.12), calls=%async_computation.1 | async-start | bytes 2097152 | tf_op jit(solution)/shard_map/all_to_all | solution.py:70
Sparse Core Ops, SparseCore 0:
  28.5 176.1 all-gather.1
where the time goes:
time: 371 us
  waiting for transfers between devices  260 us (70%)
  other arithmetic  30.6 us (8%)
  starting transfers between devices  30.1 us (8%)
  local copies, waits for them, and re-layouts  27.6 us (7%)
  between operations  13.6 us (4%)
  matrix products  8.92 us (2%)
    all_to_all x1, waiting for transfers between devices, on_device(): lax.all_to_all(sequence, 'ctx', split_axis=1, concat_axis=2, tiled=True)  233 us
    all_to_all x1, waiting for transfers between devices, on_device(): lax.all_to_all(gated, 'ctx', split_axis=1, concat_axis=0, tiled=True)  26.6 us
    add x1, other arithmetic, short_conv(): result + weights[offset][:, :, None] * padded[:, :, width - 1 - offset:wi...  24.1 us
    all_to_all x1, starting transfers between devices, on_device(): lax.all_to_all(gated, 'ctx', split_axis=1, concat_axis=0, tiled=True)  18.8 us
    convert_element_type x2, local copies, waits for them, and re-layouts, on_device(): values = spread.astype(jnp.float32)  13.5 us
    all_to_all x1, starting transfers between devices, on_device(): lax.all_to_all(sequence, 'ctx', split_axis=1, concat_axis=2, tiled=True)  11.3 us
    unnamed x8, local copies, waits for them, and re-layouts  9 us
  transfers between devices with their start and end apart: 3, of which 2 were waited for; matrix products, arithmetic and copies ran while one was open for 14% of the time, Pallas kernels for 0%

commit v1 on v0

v1 whole, which is shorter than its diff:
```python
import functools

import jax
import jax.numpy as jnp
from jax import lax
from jax.experimental import pallas as pl
from jax.experimental.pallas import tpu as pltpu
from jax.sharding import PartitionSpec as P

MESH = pl.DeviceIdType.MESH
F32, BF16 = jnp.float32, jnp.bfloat16
T = 256
C = 128
TILES = 16
TAPS = 7
LF = 128
VMEM_BYTES = 56 * 1024 * 1024
BATCH = 4

SCHEDULE = (
    ("zdirect",), ("P1", 0), ("A", 0), ("S1", 0), ("zf1",), ("P1", 1), ("A", 1), ("S1", 1), ("W", 2),
    ("P1", 2), ("A", 2), ("zf3",), ("P1", 3), ("S2", 0), ("A", 3), ("S2", 1), ("S1", 2), ("B", 0), ("S1", 3),
    ("B", 1), ("S2", 2), ("B", 2), ("S2", 3), ("B", 3), ("M", 0), ("M", 1), ("M", 2), ("M", 3),
)


def kernel(x_ref, taps_hbm, filt_hbm, w_ref, o_ref,
           taps_ref, filt_ref, buf, xs, xt, wt, fr, toe, zs, qs, head, tail, halo, gs, acc, stage,
           ss, rs, lsem, hs, hr, gsend, grecv, osend, orecv, olocal):
    f = lax.axis_index("fsdp")
    c = lax.axis_index("ctx")
    zh, x = f // 4, f % 4
    zl, y, k = c // 8, (c // 2) % 4, c % 2
    z = zh * 4 + zl

    def at(x, y, z, k):
        return ((z // 4) * 4 + x, ((z % 4) * 4 + y) * 2 + k)

    def xy(dp, ds):
        return at((x + dp + (ds - dp) * k) % 4, (y + ds + (dp - ds) * k) % 4, z, k)

    def zz(d):
        return at(x, y, (z + d + 16) % 16, k)

    sibling = at(x, y, z, 1 - k)
    before, after = (f, (c + 31) % 32), (f, (c + 1) % 32)
    inner = ((zl + 1) // 2) % 2
    edge = inner == 0
    sg = (zl // 3) * 2 - 1
    pair = 1 - 2 * (zl % 2)
    srcd = -pair * (1 + 2 * inner)
    first, last = c == 0, c == 31

    def remote(src, dst, s, r, dev):
        return pltpu.make_async_remote_copy(
            src_ref=src, dst_ref=dst, send_sem=s, recv_sem=r, device_id=dev, device_id_type=MESH
        )

    barrier = pltpu.get_barrier_semaphore()

    def sig(d):
        pl.semaphore_signal(barrier, inc=1, device_id=d, device_id_type=MESH)

    for d in (xy(1, 0), xy(3, 0), xy(2, 0), xy(0, 1), xy(0, 3), zz(pair), zz(srcd), sibling):
        sig(d)
    pl.when(edge)(lambda: sig(zz(5 * sg)))
    pl.when(jnp.logical_not(first))(lambda: sig(before))

    def load(b):
        rows = pl.ds(b * BATCH * C, BATCH * C)
        return pltpu.make_async_copy(x_ref.at[0, :, rows], xs.at[:, rows], lsem.at[b])

    own = pltpu.make_async_copy(
        w_ref.at[:, pl.ds(pl.multiple_of(k * 1024 + y * 256, 256), 256)], buf.at[0, 0, 0], lsem.at[4]
    )
    small = (
        pltpu.make_async_copy(filt_hbm, filt_ref, lsem.at[5]),
        pltpu.make_async_copy(taps_hbm, taps_ref, lsem.at[6]),
    )
    own.start()
    for cp in small:
        cp.start()
    for b in range(4):
        load(b).start()
    for cp in small:
        cp.wait()

    for m in range(3):
        row = taps_ref[m].astype(F32)
        for ct in range(TILES):
            wt[ct, 8 * m : 8 * m + TAPS, :] = row[:, ct * C : (ct + 1) * C]
    r_i = lax.broadcasted_iota(jnp.int32, (LF, LF), 0)
    c_i = lax.broadcasted_iota(jnp.int32, (LF, LF), 1)
    flip = jnp.where((r_i + c_i) % LF == 0, 1.0, 0.0).astype(BF16)
    fr[...] = jnp.dot(filt_ref[...], flip, preferred_element_type=F32)

    def build(ct, _):
        rows = fr[pl.ds(pl.multiple_of(ct * 8, 8), 8), :]
        for g in range(8):
            wide = jnp.broadcast_to(rows[g : g + 1, :], (LF, LF))
            turned = pltpu.roll(wide, 0, 1, stride=1, stride_axis=0)
            toe[ct, :, 256 * g : 256 * g + 128] = jnp.where(r_i < c_i, turned, 0.0).astype(BF16)
            toe[ct, :, 256 * g + 128 : 256 * g + 256] = jnp.where(r_i >= c_i, turned, 0.0).astype(BF16)
        return 0

    lax.fori_loop(0, TILES, build, 0)
    xt[:, 0:16, :] = jnp.zeros((3, 16, C), F32)

    def empty():
        halo[...] = jnp.zeros(halo.shape, BF16)
        zs[:, 0:LF, :] = jnp.zeros((TILES, LF, C), BF16)

    pl.when(first)(empty)
    own.wait()
    pl.semaphore_wait(barrier, 7 + 3 * (1 - inner) + jnp.where(last, 0, 1))

    sent = []
    count = [0] * 4

    def send(src, dst, dev, o):
        cp = remote(buf.at[src], buf.at[dst], ss.at[o, count[o]], rs.at[dst], dev)
        count[o] += 1
        cp.start()
        sent.append(cp)

    def got(slot):
        remote(buf.at[slot], buf.at[slot], ss.at[0, 0], rs.at[slot], sibling).wait_recv()

    far = ((1, 1, 13), (3, 1, 14), (5, 3, 15))

    def zdirect():
        def go():
            for m, o, n in far:
                remote(buf.at[0, 0, 0], buf.at[o, 0, 0], ss.at[0, n], rs.at[o, 0, 0], zz(m * sg)).start()

        pl.when(edge)(go)

    def P1(o):
        for dp, slot in ((1, 3), (3, 1), (2, 2)):
            send((o, 0, 0), (o, 0, slot), xy(dp, 0), o)
        for ds, slot in ((1, 3), (3, 1)):
            send((o, 0, 0), (o, slot, 0), xy(0, ds), o)

    def S1(o):
        for p in (1, 3, 2):
            got((o, 0, p))
            for ds, slot in ((1, 3), (3, 1)):
                send((o, 0, p), (o, slot, p), xy(0, ds), o)

    def S2(o):
        for sl, p, ds in ((3, 0, 1), (1, 3, 3), (3, 1, 1), (1, 2, 3)):
            got((o, sl, p))
            send((o, sl, p), (o, 2, p), xy(0, ds), o)

    def F(o):
        for s in ((3, 2), (3, 3), (1, 0), (1, 1), (2, 0), (2, 1), (2, 2), (2, 3)):
            got((o,) + s)

    def zf1():
        got((1, 0, 0))
        send((1, 0, 0), (2, 0, 0), zz(pair), 1)

    def zf3():
        got((3, 0, 0))

        def go():
            remote(buf.at[3, 0, 0], buf.at[3, 0, 0], ss.at[3, 15], rs.at[3, 0, 0], zz(pair)).start()

        pl.when(edge)(go)

    def halo_copies(b):
        tiles = pl.ds(b * BATCH, BATCH)
        return (
            remote(tail.at[tiles], halo.at[tiles], hs.at[b, 0], hr.at[b, 0], after),
            remote(zs.at[tiles, pl.ds(256, LF)], zs.at[tiles, pl.ds(0, LF)], hs.at[b, 1], hr.at[b, 1], after),
        )

    def conv(ct, m, r0, rows):
        total = wt[ct, 8 * m : 8 * m + 1, :] * xt[m, r0 : r0 + rows, :]
        for j in range(1, TAPS):
            total = total + wt[ct, 8 * m + j : 8 * m + j + 1, :] * xt[m, r0 - j : r0 - j + rows, :]
        return total

    def A(b):
        load(b).wait()

        def body(ct, _):
            chans = pl.ds(pl.multiple_of(ct * C, C), C)
            for m in range(3):
                turned = jnp.transpose(xs[m, chans, :])
                tail[ct, m] = turned[T - 16 :, :]
                wide = turned.astype(F32)
                head[ct, m] = wide[:16]
                xt[m, 16 : 16 + T, :] = wide
            for r in range(0, T, 64):
                zs[ct, LF + r : LF + r + 64, :] = (conv(ct, 1, 16 + r, 64) * conv(ct, 2, 16 + r, 64)).astype(BF16)
                qs[ct, r : r + 64, :] = conv(ct, 0, 16 + r, 64)
            return 0

        lax.fori_loop(b * BATCH, (b + 1) * BATCH, body, 0)

        def go():
            for cp in halo_copies(b):
                cp.start()

        pl.when(jnp.logical_not(last))(go)

    lane = lax.broadcasted_iota(jnp.int32, (1, 256), 1)
    masks = [jnp.where((lane // 16) % 8 == g, 1.0, 0.0).astype(BF16) for g in range(8)]
    mine = pl.ds(pl.multiple_of(k * T, T), T)
    other = pl.ds(pl.multiple_of((1 - k) * T, T), T)

    def B(b):
        def come():
            for cp in halo_copies(b):
                cp.wait_recv()

        pl.when(jnp.logical_not(first))(come)

        def body(ct, _):
            for m in range(3):
                xt[m, 0:16, :] = halo[ct, m].astype(F32)
                xt[m, 16:32, :] = head[ct, m]
            zs[ct, LF : LF + 16, :] = (conv(ct, 1, 16, 16) * conv(ct, 2, 16, 16)).astype(BF16)
            qs[ct, 0:16, :] = conv(ct, 0, 16, 16)
            both = jnp.concatenate([zs[ct, 0:256, :], zs[ct, 128:384, :]], axis=1)
            total = jnp.zeros((LF, 256), F32)
            for g in range(8):
                total = total + jnp.dot(
                    toe[ct, :, 256 * g : 256 * g + 256], both * masks[g], preferred_element_type=F32
                )
            for h in range(2):
                gated = (qs[ct, 128 * h : 128 * h + 128, :] * total[:, 128 * h : 128 * h + 128]).astype(BF16)
                gs[ct, pl.ds(pl.multiple_of(k * T + 128 * h, 128), 128), :] = gated
            return 0

        lax.fori_loop(b * BATCH, (b + 1) * BATCH, body, 0)
        tiles = pl.ds(b * BATCH, BATCH)
        remote(gs.at[tiles, mine], gs.at[tiles, mine], gsend.at[b], grecv.at[b], sibling).start()

    def source(o):
        if o == 0:
            return zh
        if o == 3:
            return (zh + 2) % 4
        return (zh + 4 - pair * (3 - 2 * o)) % 4

    def out_copies(j):
        n = (y + j) % 4
        cols = pl.ds(pl.multiple_of(k * 1024 + n * 256, 256), 256)
        return (
            remote(stage.at[j, other], o_ref.at[:, cols], osend.at[j], orecv.at[j], sibling),
            pltpu.make_async_copy(stage.at[j, mine], o_ref.at[:, cols], olocal.at[j]),
        )

    def M(o):
        F(o)
        if o == 0:
            for b in range(4):
                tiles = pl.ds(b * BATCH, BATCH)
                remote(gs.at[tiles, other], gs.at[tiles, other], gsend.at[b], grecv.at[b], sibling).wait_recv()
        part = source(o) * 4
        left = jnp.concatenate([gs[part + (x + i) % 4] for i in range(4)], axis=1)
        for j in range(4):
            right = jnp.concatenate(
                [buf[o, j + (i - j) * k, i + (j - i) * k] for i in range(4)], axis=0
            )
            product = jnp.dot(left, right, preferred_element_type=F32)
            if o == 0:
                acc[j] = product
            elif o < 3:
                acc[j] += product
            else:
                stage[j] = (acc[j] + product).astype(BF16)
                for cp in out_copies(j):
                    cp.start()

    names = dict(P1=P1, S1=S1, S2=S2, A=A, B=B, M=M, zdirect=zdirect, zf1=zf1, zf3=zf3, W=lambda o: got((o, 0, 0)))
    for name, *arguments in SCHEDULE:
        names[name](*arguments)

    for cp in sent:
        cp.wait_send()

    def far_sent():
        for o, n in ((0, 13), (0, 14), (0, 15), (3, 15)):
            remote(buf.at[0, 0, 0], buf.at[0, 0, 0], ss.at[o, n], rs.at[0, 0, 0], sibling).wait_send()

    pl.when(edge)(far_sent)

    def halo_sent():
        for b in range(4):
            for cp in halo_copies(b):
                cp.wait_send()

    pl.when(jnp.logical_not(last))(halo_sent)
    for b in range(4):
        tiles = pl.ds(b * BATCH, BATCH)
        remote(gs.at[tiles, mine], gs.at[tiles, mine], gsend.at[b], grecv.at[b], sibling).wait_send()
    for j in range(4):
        there, here = out_copies(j)
        there.wait_send()
        here.wait()
    for j in range(4):
        n = (y + j) % 4
        cols = pl.ds(pl.multiple_of((1 - k) * 1024 + n * 256, 256), 256)
        remote(stage.at[j, other], o_ref.at[:, cols], osend.at[j], orecv.at[j], sibling).wait_recv()


def on_device(features, short_taps, filters, out_weight):
    dma = pltpu.SemaphoreType.DMA
    any_space = pl.BlockSpec(memory_space=pl.ANY)
    out = pl.pallas_call(
        kernel,
        out_shape=jax.ShapeDtypeStruct((T, 2048), BF16),
        in_specs=[pl.BlockSpec(memory_space=pltpu.HBM)] * 4,
        out_specs=any_space,
        scratch_shapes=[
            pltpu.VMEM((3, TAPS, 2048), BF16),
            pltpu.VMEM((LF, LF), BF16),
            pltpu.VMEM((4, 4, 4, C, 256), BF16),
            pltpu.VMEM((3, 2048, T), BF16),
            pltpu.VMEM((3, T + 16, C), F32),
            pltpu.VMEM((TILES, 24, C), F32),
            pltpu.VMEM((LF, LF), F32),
            pltpu.VMEM((TILES, LF, 8 * 256), BF16),
            pltpu.VMEM((TILES, LF + T, C), BF16),
            pltpu.VMEM((TILES, T, C), F32),
            pltpu.VMEM((TILES, 3, 16, C), F32),
            pltpu.VMEM((TILES, 3, 16, C), BF16),
            pltpu.VMEM((TILES, 3, 16, C), BF16),
            pltpu.VMEM((TILES, 2 * T, C), BF16),
            pltpu.VMEM((4, 2 * T, 256), F32),
            pltpu.VMEM((4, 2 * T, 256), BF16),
            dma((4, 17)), dma((4, 4, 4)), dma((7,)), dma((4, 2)), dma((4, 2)),
            dma((4,)), dma((4,)), dma((4,)), dma((4,)), dma((4,)),
        ],
        compiler_params=pltpu.CompilerParams(
            collective_id=0, has_side_effects=True, vmem_limit_bytes=VMEM_BYTES
        ),
        name="hyena",
    )(features, jnp.transpose(short_taps, (1, 0, 2)), filters, out_weight)
    return out[None]


def solution(mesh):
    in_specs = (P("fsdp", None, None, "ctx"), P(), P(), P("fsdp", None))
    return jax.shard_map(
        on_device, mesh=mesh, in_specs=in_specs, out_specs=P("fsdp", "ctx", None), check_vma=False
    )
```

time: 371 us -> 54 us (0.15)
  waiting for transfers between devices: 260 us -> 0 us
  Pallas kernels: 0 us -> 51.5 us
  other arithmetic: 30.6 us -> 0 us
  starting transfers between devices: 30.1 us -> 0 us
  local copies, waits for them, and re-layouts: 27.6 us -> 2.3 us
  between operations: 13.6 us -> 0.01 us
  matrix products: 8.92 us -> 0 us
    all_to_all x2 -> x0, waiting for transfers between devices: 259 us -> none  [the longest x1 233 us: on_device(): lax.all_to_all(sequence, 'ctx', split_axis=1, concat_axis=2, tiled=True)]
    pallas_call x0 -> x1, Pallas kernels: none -> 51.5 us  [on_device(): pl.pallas_call(kernel, out_shape=jax.ShapeDtypeStruct((T, 2048), BF16), i...]
    all_to_all x2 -> x0, starting transfers between devices: 30.1 us -> none  [the longest x1 18.8 us: on_device(): lax.all_to_all(gated, 'ctx', split_axis=1, concat_axis=0, tiled=True)]
    add x1 -> x0, other arithmetic: 24.1 us -> none  [short_conv(): result + weights[offset][:, :, None] * padded[:, :, width - 1 - offset:wi...]
    convert_element_type x3 -> x0, local copies, waits for them, and re-layouts: 15 us -> none  [the longest x2 13.5 us: on_device(): values = spread.astype(jnp.float32)]
    dot_general x3 -> x0, matrix products: 8.92 us -> none  [the longest x1 6.7 us: on_device(): lax.dot_general(mixed, lax.all_gather(out_weight, 'fsdp', axis=0, tiled=T...]
    unnamed x8 -> x1, local copies, waits for them, and re-layouts: 9 us -> 2.3 us
    convert_element_type x3 -> x0, other arithmetic: 4.72 us -> none  [the longest x1 3.43 us: on_device(): values = spread.astype(jnp.float32)]
  transfers between devices with their start and end apart: 3 -> 0, of which waited for: 2 -> 0; matrix products, arithmetic and copies ran while one was open for 14% -> 0% of each run, Pallas kernels for 0% -> 0%
where the time goes in v1:
time: 54 us; the launch traced here: 53.9 us
  Pallas kernels  51.5 us (95%)
  local copies, waits for them, and re-layouts  2.3 us (4%)
    pallas_call x1, Pallas kernels, on_device(): pl.pallas_call(kernel, out_shape=jax.ShapeDtypeStruct((T, 2048), BF16), i...  51.5 us
    unnamed x1, local copies, waits for them, and re-layouts  2.3 us

profile of v1, /device:TPU:1, one launch (start us, length us, event | category | flops | bytes accessed | tf_op | source)
XLA Modules:
  0.0 53.9 jit_solution(15688148476775657132)
XLA Ops:
  0.0 51.5 %hyena.1 = bf16[256,2048]{1,0:T(8,128)(2,1)} custom-call(bf16[1,3,2048,256]{3,2,1,0:T(8,128)(2,1)} %x_ref.1, bf16[3,7,2048]{2,1,0:T(8,128)(2,1)} %bitcast.3, bf16[128,128]{1,0:T(8,128)(2,1)} %filt_hbm.1, bf16[128,2048]{1,0:T(8,128)(2,1)} %w_ref.1), custom_call_target="tpu_custom_call" | custom-call | tf_op jit(solution)/shard_map/hyena/pallas_call | solution.py:313
  51.6 2.3 %copy.6 = bf16[1,256,2048]{2,1,0:T(8,128)(2,1)} copy(bf16[1,256,2048]{2,1,0:T(8,128)(2,1)} %bitcast.2) | data formatting | bytes 2097152

commit v2 on v1

--- a/solution.py
+++ b/solution.py
@@ -19,14 +19,15 @@
 
 SCHEDULE = (
     ("zdirect",), ("P1", 0), ("A", 0), ("S1", 0), ("zf1",), ("P1", 1), ("A", 1), ("S1", 1), ("W", 2),
-    ("P1", 2), ("A", 2), ("zf3",), ("P1", 3), ("S2", 0), ("A", 3), ("S2", 1), ("S1", 2), ("B", 0), ("S1", 3),
-    ("B", 1), ("S2", 2), ("B", 2), ("S2", 3), ("B", 3), ("M", 0), ("M", 1), ("M", 2), ("M", 3),
+    ("P1", 2), ("A", 2), ("zf3",), ("P1", 3), ("S2", 0), ("Q", 2), ("A", 3), ("S2", 1), ("S1", 2), ("Q", 0),
+    ("Q", 1), ("B", 0), ("S1", 3), ("B", 1), ("S2", 2), ("B", 2), ("S2", 3), ("B", 3), ("M", 1), ("M", 0),
+    ("M", 2), ("M", 3),
 )
 
 
 def kernel(x_ref, taps_hbm, filt_hbm, w_ref, o_ref,
            taps_ref, filt_ref, buf, xs, xt, wt, fr, toe, zs, qs, head, tail, halo, gs, acc, stage,
-           ss, rs, lsem, hs, hr, gsend, grecv, osend, orecv, olocal):
+           ss, rs, sq, rq, lsem, hs, hr, gsend, grecv, osend, orecv, olocal):
     f = lax.axis_index("fsdp")
     c = lax.axis_index("ctx")
     zh, x = f // 4, f % 4
@@ -117,14 +118,25 @@
     sent = []
     count = [0] * 4
 
+    half = pl.ds(pl.multiple_of(zl % 2 * 64, 64), 64)
+    rest = pl.ds(pl.multiple_of((1 - zl % 2) * 64, 64), 64)
+
+    def piece(slot):
+        return buf.at[(*slot, half)] if slot[0] == 0 else buf.at[slot]
+
     def send(src, dst, dev, o):
-        cp = remote(buf.at[src], buf.at[dst], ss.at[o, count[o]], rs.at[dst], dev)
+        cp = remote(piece(src), piece(dst), ss.at[o, count[o]], rs.at[dst], dev)
         count[o] += 1
         cp.start()
         sent.append(cp)
 
     def got(slot):
-        remote(buf.at[slot], buf.at[slot], ss.at[0, 0], rs.at[slot], sibling).wait_recv()
+        remote(piece(slot), piece(slot), ss.at[0, 0], rs.at[slot], sibling).wait_recv()
+
+    def share(s, p):
+        cp = remote(buf.at[0, s, p, half], buf.at[0, s, p, half], sq.at[s, p], rq.at[s, p], zz(pair))
+        cp.start()
+        sent.append(cp)
 
     far = ((1, 1, 13), (3, 1, 14), (5, 3, 15))
 
@@ -152,9 +164,27 @@
             got((o, sl, p))
             send((o, sl, p), (o, 2, p), xy(0, ds), o)
 
+    late = ((3, 2), (3, 3), (1, 0), (1, 1), (2, 0), (2, 1), (2, 2), (2, 3))
+
+    def Q(some):
+        if some == 2:
+            for s, p in ((0, 1), (0, 3), (0, 2), (3, 0), (1, 3), (3, 1), (1, 2)):
+                share(s, p)
+            return
+        for s, p in late[:4] if some == 0 else late[4:]:
+            got((0, s, p))
+            share(s, p)
+
     def F(o):
-        for s in ((3, 2), (3, 3), (1, 0), (1, 1), (2, 0), (2, 1), (2, 2), (2, 3)):
-            got((o,) + s)
+        if o > 0:
+            for s in late:
+                got((o,) + s)
+            return
+        for s in range(4):
+            for p in range(4):
+                if s or p:
+                    theirs = buf.at[0, s, p, rest]
+                    remote(theirs, theirs, sq.at[s, p], rq.at[s, p], sibling).wait_recv()
 
     def zf1():
         got((1, 0, 0))
@@ -197,7 +227,7 @@
                 qs[ct, r : r + 64, :] = conv(ct, 0, 16 + r, 64)
             return 0
 
-        lax.fori_loop(b * BATCH, (b + 1) * BATCH, body, 0)
+        lax.fori_loop(b * BATCH, (b + 1) * BATCH, body, 0, unroll=2)
 
         def go():
             for cp in halo_copies(b):
@@ -234,7 +264,7 @@
                 gs[ct, pl.ds(pl.multiple_of(k * T + 128 * h, 128), 128), :] = gated
             return 0
 
-        lax.fori_loop(b * BATCH, (b + 1) * BATCH, body, 0)
+        lax.fori_loop(b * BATCH, (b + 1) * BATCH, body, 0, unroll=2)
         tiles = pl.ds(b * BATCH, BATCH)
         remote(gs.at[tiles, mine], gs.at[tiles, mine], gsend.at[b], grecv.at[b], sibling).start()
 
@@ -255,7 +285,7 @@
 
     def M(o):
         F(o)
-        if o == 0:
+        if o == 1:
             for b in range(4):
                 tiles = pl.ds(b * BATCH, BATCH)
                 remote(gs.at[tiles, other], gs.at[tiles, other], gsend.at[b], grecv.at[b], sibling).wait_recv()
@@ -266,7 +296,7 @@
                 [buf[o, j + (i - j) * k, i + (j - i) * k] for i in range(4)], axis=0
             )
             product = jnp.dot(left, right, preferred_element_type=F32)
-            if o == 0:
+            if o == 1:
                 acc[j] = product
             elif o < 3:
                 acc[j] += product
@@ -275,7 +305,7 @@
                 for cp in out_copies(j):
                     cp.start()
 
-    names = dict(P1=P1, S1=S1, S2=S2, A=A, B=B, M=M, zdirect=zdirect, zf1=zf1, zf3=zf3, W=lambda o: got((o, 0, 0)))
+    names = dict(Q=Q, P1=P1, S1=S1, S2=S2, A=A, B=B, M=M, zdirect=zdirect, zf1=zf1, zf3=zf3, W=lambda o: got((o, 0, 0)))
     for name, *arguments in SCHEDULE:
         names[name](*arguments)
 
@@ -332,7 +362,7 @@
             pltpu.VMEM((TILES, 2 * T, C), BF16),
             pltpu.VMEM((4, 2 * T, 256), F32),
             pltpu.VMEM((4, 2 * T, 256), BF16),
-            dma((4, 17)), dma((4, 4, 4)), dma((7,)), dma((4, 2)), dma((4, 2)),
+            dma((4, 17)), dma((4, 4, 4)), dma((4, 4)), dma((4, 4)), dma((7,)), dma((4, 2)), dma((4, 2)),
             dma((4,)), dma((4,)), dma((4,)), dma((4,)), dma((4,)),
         ],
         compiler_params=pltpu.CompilerParams(

time: 54 us -> 52.8 us (0.978)
  Pallas kernels: 51.5 us -> 50.1 us
    pallas_call x1, Pallas kernels: 51.5 us -> 50.1 us  [on_device(): pl.pallas_call(kernel, out_shape=jax.ShapeDtypeStruct((T, 2048), BF16), i...]
where the time goes in v2:
time: 52.8 us; the launch traced here: 52.4 us
  Pallas kernels  50.1 us (95%)
  local copies, waits for them, and re-layouts  2.3 us (4%)
    pallas_call x1, Pallas kernels, on_device(): pl.pallas_call(kernel, out_shape=jax.ShapeDtypeStruct((T, 2048), BF16), i...  50.1 us
    unnamed x1, local copies, waits for them, and re-layouts  2.3 us

profile of v2, /device:TPU:1, one launch (start us, length us, event | category | flops | bytes accessed | tf_op | source)
XLA Modules:
  0.0 52.4 jit_solution(6529940600869000884)
XLA Ops:
  0.0 50.1 %hyena.1 = bf16[256,2048]{1,0:T(8,128)(2,1)} custom-call(bf16[1,3,2048,256]{3,2,1,0:T(8,128)(2,1)} %x_ref.1, bf16[3,7,2048]{2,1,0:T(8,128)(2,1)} %bitcast.3, bf16[128,128]{1,0:T(8,128)(2,1)} %filt_hbm.1, bf16[128,2048]{1,0:T(8,128)(2,1)} %w_ref.1), custom_call_target="tpu_custom_call" | custom-call | tf_op jit(solution)/shard_map/hyena/pallas_call | solution.py:343
  50.1 2.3 %copy.6 = bf16[1,256,2048]{2,1,0:T(8,128)(2,1)} copy(bf16[1,256,2048]{2,1,0:T(8,128)(2,1)} %bitcast.2) | data formatting | bytes 2097152

commit v3 on v2

--- a/solution.py
+++ b/solution.py
@@ -18,8 +18,8 @@
 BATCH = 4
 
 SCHEDULE = (
-    ("zdirect",), ("P1", 0), ("A", 0), ("S1", 0), ("zf1",), ("P1", 1), ("A", 1), ("S1", 1), ("W", 2),
-    ("P1", 2), ("A", 2), ("zf3",), ("P1", 3), ("S2", 0), ("Q", 2), ("A", 3), ("S2", 1), ("S1", 2), ("Q", 0),
+    ("zdirect",), ("P1", 0), ("A", 0), ("S1", 0), ("zf1",), ("P1", 1), ("A", 1), ("S1", 1), ("A", 2),
+    ("W", 2), ("P1", 2), ("zf3",), ("P1", 3), ("S2", 0), ("Q", 2), ("A", 3), ("S2", 1), ("S1", 2), ("Q", 0),
     ("Q", 1), ("B", 0), ("S1", 3), ("B", 1), ("S2", 2), ("B", 2), ("S2", 3), ("B", 3), ("M", 1), ("M", 0),
     ("M", 2), ("M", 3),
 )

time: 52.8 us -> 53.4 us (1.011); the launches traced: 52.4 us -> 52.4 us
  no operation moved by 1% of the time
where the time goes in v3:
time: 53.4 us; the launch traced here: 52.4 us
  Pallas kernels  50.1 us (94%)
  local copies, waits for them, and re-layouts  2.3 us (4%)
    pallas_call x1, Pallas kernels, on_device(): pl.pallas_call(kernel, out_shape=jax.ShapeDtypeStruct((T, 2048), BF16), i...  50.1 us
    unnamed x1, local copies, waits for them, and re-layouts  2.3 us

profile of v3, /device:TPU:1, one launch (start us, length us, event | category | flops | bytes accessed | tf_op | source)
XLA Modules:
  0.0 52.4 jit_solution(17190801784953844284)
XLA Ops:
  0.0 50.1 %hyena.1 = bf16[256,2048]{1,0:T(8,128)(2,1)} custom-call(bf16[1,3,2048,256]{3,2,1,0:T(8,128)(2,1)} %x_ref.1, bf16[3,7,2048]{2,1,0:T(8,128)(2,1)} %bitcast.3, bf16[128,128]{1,0:T(8,128)(2,1)} %filt_hbm.1, bf16[128,2048]{1,0:T(8,128)(2,1)} %w_ref.1), custom_call_target="tpu_custom_call" | custom-call | tf_op jit(solution)/shard_map/hyena/pallas_call | solution.py:343
  50.1 2.3 %copy.6 = bf16[1,256,2048]{2,1,0:T(8,128)(2,1)} copy(bf16[1,256,2048]{2,1,0:T(8,128)(2,1)} %bitcast.2) | data formatting | bytes 2097152
